TPU v7x, 512 devices: a whole 4x8x8 slice. The times are simulated.
512 devices in a mesh: dp: 4 (over x), seq: 64 (over y, z), tensor: 2 (over core).
Axes of the slice: x: 4, y: 8, z: 8, core: 2. Of those that a mesh axis runs over, the one named last changes fastest.
Arguments:
- q_raw: bfloat16 [4, 24576, 1536], P('dp', 'seq', 'tensor')
- k_raw: bfloat16 [4, 24576, 1536], P('dp', 'seq', 'tensor')
- values: bfloat16 [4, 24576, 1536], P('dp', 'seq', 'tensor'), may hold values from -6 to 6
- d_out: bfloat16 [4, 24576, 1536], P('dp', 'seq', 'tensor')
- gain_q: float32 [128], replicated, may hold values from 0.5 to 4.5
- gain_k: float32 [128], replicated, may hold values from 0.5 to 4.5
- tile_lists: int32 [4, 64, 3], P('dp'), may hold values from 0 to 63, as said below
- tile_counts: int32 [4, 64], P('dp'), may hold values from 1 to 3, as said below
Outputs:
- grad_q_raw: bfloat16 [4, 24576, 1536], P('dp', 'seq', 'tensor')
- grad_k_raw: bfloat16 [4, 24576, 1536], P('dp', 'seq', 'tensor')
- grad_values: bfloat16 [4, 24576, 1536], P('dp', 'seq', 'tensor')
- grad_gain_q: float32 [128], replicated
- grad_gain_k: float32 [128], replicated
Inputs may be any that keep to these rules, and one draw needn't show every extreme that they name: `tile_lists`: entry 0 of row a is a itself; the next entries up to the count are distinct tiles that share a face with a in the grid of 16 x 2 x 2 tiles, where tile index = (t * 2 + h) * 2 + w; entries past the count equal a. `tile_counts`: some tile of each clip attends 3 tiles.
All inputs are finite; a program needn't handle non-finite values.
Results may differ from a plain program's by a relative error of at most 0.0085.
The roundings to bfloat16 on the way count: a program that leaves them out, or rounds other values in their place, can miss the bound.
Values may be sent and summed in bfloat16 or wider, within the bound.
A program may use at most 128 MiB of HBM per device.

v0:
```python
import jax
import jax.numpy as jnp
from jax import lax
from jax.sharding import PartitionSpec as P

TGH = 2
TGW = 2


EPS = 1e-06


def shifted(block, axis, distance):
    devices = range(lax.axis_size(axis))
    route = [(i - distance, i) for i in devices if i - distance in devices]
    return lax.ppermute(block, axis, route)


def normalize(raw, head_dim):
    wide = raw.astype(jnp.float32).reshape(raw.shape[0], -1, head_dim)
    inverse = lax.rsqrt(jnp.mean(wide * wide, axis=-1, keepdims=True) + EPS)
    return (wide * inverse, inverse)


def norm_backward(grad, normed, inverse, gain):
    scaled = grad * gain
    inner = jnp.mean(normed * scaled, axis=-1, keepdims=True)
    return ((scaled - normed * inner) * inverse, jnp.sum(grad * normed, axis=(0, 1)))


def tile_scores(query, key_tile, factor):
    return jnp.einsum("qhd,khd->hqk", query, key_tile, preferred_element_type=jnp.float32) * factor


def score_grads(query, grad_out, log_total, delta, pair, factor):
    scores = tile_scores(query, pair[0], factor)
    prob = jnp.exp(scores - log_total[..., None])
    dprob = jnp.einsum("qhd,khd->hqk", grad_out, pair[1], preferred_element_type=jnp.float32)
    dscore = (prob * (dprob - delta[..., None])).astype(jnp.bfloat16)
    return (prob, dscore)


def shards(q_raw, k_raw, values, d_out, gain_q, gain_k, tile_lists, tile_counts):
    head_dim = gain_q.shape[0]
    rows = q_raw.shape[1]
    factor = head_dim ** (-0.5)
    mine = lax.axis_index("seq")
    lists_all = tile_lists[0]
    counts_all = tile_counts[0]
    my_list = lax.dynamic_index_in_dim(lists_all, mine, 0, keepdims=False)
    my_count = lax.dynamic_index_in_dim(counts_all, mine, 0, keepdims=False)
    q_normed, q_inverse = normalize(q_raw[0], head_dim)
    k_normed, k_inverse = normalize(k_raw[0], head_dim)
    query = (q_normed * gain_q).astype(jnp.bfloat16)
    key = (k_normed * gain_k).astype(jnp.bfloat16)
    heads_here = query.shape[1]
    value = values[0].reshape(rows, heads_here, head_dim)
    grad_out = d_out[0].reshape(rows, heads_here, head_dim)
    layer_step = TGH * TGW
    offsets = (1, -1, TGW, -TGW, layer_step, -layer_step)
    offset_array = jnp.array(offsets, jnp.int32)
    offset_places = jnp.arange(1, len(offsets) + 1, dtype=jnp.int32)
    local_pair = jnp.stack([key, value])
    fetched = [local_pair]
    target_ids = mine + jnp.array((0,) + offsets, jnp.int32)
    for shift_by in offsets:
        fetched.append(shifted(local_pair, "seq", -shift_by))
    pair_stack = jnp.stack(fetched)
    slot_count = len(fetched)
    slot_ids = jnp.arange(slot_count, dtype=jnp.int32)

    def pair_of(entry):
        target = lax.dynamic_index_in_dim(my_list, entry, 0, keepdims=False)
        slot = jnp.sum(jnp.where(target_ids == target, slot_ids, 0))
        return (target, lax.dynamic_index_in_dim(pair_stack, slot, 0, keepdims=False))

    first = tile_scores(query, key, factor)
    top_first = jnp.max(first, axis=-1)
    total_first = jnp.sum(jnp.exp(first - top_first[..., None]), axis=-1)

    def gather_stats(entry, state):
        top, total = state
        target, pair = pair_of(entry)
        scores = tile_scores(query, pair[0], factor)
        new_top = jnp.maximum(top, jnp.max(scores, axis=-1))
        total = total * jnp.exp(top - new_top) + jnp.sum(
            jnp.exp(scores - new_top[..., None]), axis=-1
        )
        return (new_top, total)

    top, total = lax.fori_loop(1, my_count, gather_stats, (top_first, total_first))
    log_total = top + jnp.log(total)

    def gather_delta(entry, accum):
        target, pair = pair_of(entry)
        scores = tile_scores(query, pair[0], factor)
        prob = jnp.exp(scores - log_total[..., None])
        dprob = jnp.einsum("qhd,khd->hqk", grad_out, pair[1], preferred_element_type=jnp.float32)
        return accum + jnp.sum(prob * dprob, axis=-1)

    delta = lax.fori_loop(0, my_count, gather_delta, jnp.zeros_like(log_total))
    zero_q = jnp.zeros((rows, heads_here, head_dim), jnp.float32)

    def backward_pass(entry, state):
        grad_q, partials = state
        target, pair = pair_of(entry)
        place = jnp.sum(jnp.where(offset_array == target - mine, offset_places, 0))
        prob, dscore = score_grads(query, grad_out, log_total, delta, pair, factor)
        grad_q = grad_q + factor * jnp.einsum(
            "hqk,khd->qhd", dscore, pair[0], preferred_element_type=jnp.float32
        )
        grad_k = (
            factor * jnp.einsum("hqk,qhd->khd", dscore, query, preferred_element_type=jnp.float32)
        ).astype(jnp.bfloat16)
        grad_v = jnp.einsum(
            "hqk,qhd->khd", prob.astype(jnp.bfloat16), grad_out, preferred_element_type=jnp.float32
        ).astype(jnp.bfloat16)
        partials = lax.dynamic_update_index_in_dim(partials, jnp.stack([grad_k, grad_v]), place, 0)
        return (grad_q, partials)

    empty_terms = jnp.zeros((len(offsets) + 1, 2, rows, heads_here, head_dim), jnp.bfloat16)
    grad_query, partials = lax.fori_loop(0, my_count, backward_pass, (zero_q, empty_terms))
    key_grads = partials[0].astype(jnp.float32)
    for index, shift_by in enumerate(offsets):
        arrived = shifted(partials[index + 1], "seq", shift_by)
        key_grads = key_grads + arrived.astype(jnp.float32)
    grad_q_raw, gain_part_q = norm_backward(grad_query, q_normed, q_inverse, gain_q)
    grad_k_raw, gain_part_k = norm_backward(key_grads[0], k_normed, k_inverse, gain_k)
    gain_total_q, gain_total_k = lax.psum((gain_part_q, gain_part_k), ("dp", "seq", "tensor"))
    scale_back = (lax.axis_size("dp") * lax.axis_size("seq") * rows) ** (-0.5)
    return (
        grad_q_raw.reshape(1, rows, -1).astype(jnp.bfloat16),
        grad_k_raw.reshape(1, rows, -1).astype(jnp.bfloat16),
        key_grads[1].reshape(1, rows, -1).astype(jnp.bfloat16),
        gain_total_q * scale_back,
        gain_total_k * scale_back,
    )


def solution(mesh):
    placed = (
        P("dp", "seq", "tensor"),
        P("dp", "seq", "tensor"),
        P("dp", "seq", "tensor"),
        P("dp", "seq", "tensor"),
        P(),
        P(),
        P("dp", None, None),
        P("dp", None),
    )
    return jax.shard_map(
        shards,
        mesh=mesh,
        in_specs=placed,
        out_specs=(
            P("dp", "seq", "tensor"),
            P("dp", "seq", "tensor"),
            P("dp", "seq", "tensor"),
            P(),
            P(),
        ),
        check_vma=False,
    )
```

profile of v0, /device:TPU:1, one launch (start us, length us, event | category | flops | bytes accessed | tf_op | source)
XLA Modules:
  0.0 692.5 jit_solution(12598882995731330444)
XLA Ops:
  0.7 1.4 copy.30
  4.6 1.4 collective-permute-start
  6.0 6.5 collective-permute-start.1
  12.6 1.3 collective-permute-start.2
  13.9 6.4 collective-permute-start.3
  29.2 6.0 collective-permute-done
  35.2 10.1 %collective-permute-start.5 = (bf16[2,384,6,128]{1,3,2,0:T(8,128)(2,1)}, bf16[2,384,6,128]{1,3,2,0:T(8,128)(2,1)S(1)}, u32[]{:S(2)}, u32[]{:S(2)}) collective-permute-start(bf16[2,384,6,128]{1,3,2,0:T(8,128)(2,1)} %pad_maximum_fusion), channel_id=1, source_target_pairs={{0,8},{2,10},{4,12},{6,14},{8,16},{10,18},{12,20},{14,22},{16,24},... | collective-permute-start | bytes 3538952 | tf_op jit(solution)/shard_map/ppermute | solution.py:16
  45.3 2.4 bitcast_dynamic-update-slice_fusion.5
  47.7 2.4 bitcast_dynamic-update-slice_fusion.4
  50.2 150.7 %collective-permute-done.2 = bf16[2,384,6,128]{1,3,2,0:T(8,128)(2,1)} collective-permute-done((bf16[2,384,6,128]{1,3,2,0:T(8,128)(2,1)}, bf16[2,384,6,128]{1,3,2,0:T(8,128)(2,1)}, u32[]{:S(2)}, u32[]{:S(2)}) %collective-permute-start.2) | collective-permute-done | bytes 1179680 | tf_op jit(solution)/shard_map/ppermute | solution.py:16
  200.8 2.4 bitcast_dynamic-update-slice_fusion.3
  203.3 2.4 bitcast_dynamic-update-slice_fusion.2
  205.7 2.4 bitcast_dynamic-update-slice_fusion.1
  209.3 11.5 %copy.40 = bf16[7,2,384,6,128]{4,2,3,1,0:T(8,128)(2,1)} copy(bf16[7,2,384,6,128]{2,4,3,1,0:T(8,128)(2,1)} %bitcast_dynamic-update-slice_fusion) | data formatting | bytes 16515072
  220.8 7.3 %while.39 = (s32[]{:T(128)}, f32[6,384]{1,0:T(8,128)S(1)}, f32[6,384]{1,0:T(8,128)S(1)}, s32[]{:T(128)}, s32[3]{0:T(128)S(1)}, /*index=5*/bf16[7,2,384,6,128]{4,...) while((s32[]{:T(128)}, f32[6,384]{1,0:T(8,128)S(1)}, ...), condition=%wide.region_8.9_spmd.clone, body=%wide.region_4.8_spmd.clone.sunk | while | flops 230920736 | bytes 8377601 | solution.py:91
  222.1 1.3 fusion.90
  225.3 1.7 bitcast_reduce_fusion.2
  228.8 22.9 %while.40 = (s32[]{:T(128)}, f32[6,384]{1,0:T(8,128)S(1)}, s32[]{:T(128)}, s32[3]{0:T(128)S(1)}, bf16[7,2,384,6,128]{4,2,3,1,0:T(8,128)(2,1)}, /*index=5*/bf16[3...) while((s32[]{:T(128)}, f32[6,384]{1,0:T(8,128)S(1)}, ...), condition=%wide.region_12.13_spmd.clone, body=%wide.region_9.12_spmd.clone.sunk | while | flops 456523808 | bytes 9486629 | solution.py:101
  230.0 1.3 fusion.94
  233.2 3.5 fusion.95
  236.8 3.2 multiply_reduce_fusion.7
  241.2 1.3 fusion.94
  244.4 3.5 fusion.95
  248.0 3.2 multiply_reduce_fusion.7
  252.9 4.5 broadcast_in_dim.41.clone
  257.4 41.3 %while.41 = (s32[]{:T(128)}, f32[384,6,128]{0,2,1:T(8,128)}, bf16[7,2,384,6,128]{2,4,3,1,0:T(8,128)(2,1)}, s32[]{:T(128)}, s32[3]{0:T(128)S(1)}, /*index=5*/bf16...) while((s32[]{:T(128)}, f32[384,6,128]{0,2,1:T(8,128)}, ...), condition=%wide.region_16.17_spmd.clone.clone.clone, body=%wide.region_13.16_spmd.sunk.clone.clone.clone.sunk | while | flops 1141604352 | bytes 44858132 | solution.py:122
  259.0 1.3 fusion.103
  262.3 1.9 fusion.104
  264.2 2.3 multiply_convert_fusion.7
  266.5 2.1 fusion.105
  268.6 2.3 fusion.106
  270.9 1.7 fusion.107
  279.3 1.3 fusion.103
  282.7 1.9 fusion.104
  284.5 2.3 multiply_convert_fusion.7
  286.9 2.0 fusion.105
  288.9 2.3 fusion.106
  291.2 1.7 fusion.107
  298.8 5.5 slice_bitcast_fusion.5
  305.6 8.9 %collective-permute-start.10 = (bf16[2,384,6,128]{1,3,2,0:T(8,128)(2,1)}, bf16[2,384,6,128]{1,3,2,0:T(8,128)(2,1)}, u32[]{:S(2)}, u32[]{:S(2)}) collective-permute-start(bf16[2,384,6,128]{1,3,2,0:T(8,128)(2,1)} %get-tuple-element.466), channel_id=1, source_target_pairs={{0,8},{2,10},{4,12},{6,14},{8,16},{10,18},{12,20},{14,22},{16,24},... | collective-permute-start | bytes 3538952 | tf_op jit(solution)/shard_map/ppermute | solution.py:16
  315.8 5.9 collective-permute-start.8
  323.0 36.0 %collective-permute-done.11 = bf16[2,384,6,128]{1,3,2,0:T(8,128)(2,1)S(1)} collective-permute-done((bf16[2,384,6,128]{1,3,2,0:T(8,128)(2,1)S(1)}, bf16[2,384,6,128]{1,3,2,0:T(8,128)(2,1)S(1)}, u32[]{:S(2)}, u32[]{:S(2)}) %collective-permute-start.11) | collective-permute-done | bytes 1179680 | tf_op jit(solution)/shard_map/ppermute | solution.py:16
  359.0 24.9 %collective-permute-start.6 = (bf16[2,384,6,128]{1,3,2,0:T(8,128)(2,1)S(1)}, bf16[2,384,6,128]{1,3,2,0:T(8,128)(2,1)}, u32[]{:S(2)}, u32[]{:S(2)}) collective-permute-start(bf16[2,384,6,128]{1,3,2,0:T(8,128)(2,1)S(1)} %get-tuple-element.465), channel_id=1, source_target_pairs={{0,2},{2,4},{4,6},{6,8},{8,10},{10,12},{12,14},{14,16},{16,18},{18... | collective-permute-start | bytes 3538952 | tf_op jit(solution)/shard_map/ppermute | solution.py:16
  385.7 4.4 collective-permute-done.10
  390.0 80.1 %collective-permute-done.9 = bf16[2,384,6,128]{1,3,2,0:T(8,128)(2,1)} collective-permute-done((bf16[2,384,6,128]{1,3,2,0:T(8,128)(2,1)}, bf16[2,384,6,128]{1,3,2,0:T(8,128)(2,1)}, u32[]{:S(2)}, u32[]{:S(2)}) %collective-permute-start.9) | collective-permute-done | bytes 1179680 | tf_op jit(solution)/shard_map/ppermute | solution.py:16
  470.1 41.9 %collective-permute-done.7 = bf16[2,384,6,128]{1,3,2,0:T(8,128)(2,1)} collective-permute-done((bf16[2,384,6,128]{1,3,2,0:T(8,128)(2,1)S(1)}, bf16[2,384,6,128]{1,3,2,0:T(8,128)(2,1)}, u32[]{:S(2)}, u32[]{:S(2)}) %collective-permute-start.7) | collective-permute-done | bytes 1179680 | tf_op jit(solution)/shard_map/ppermute | solution.py:16
  512.0 4.7 fusion.49
  521.9 170.1 %all-reduce = (f32[128]{0:T(128)S(1)}, f32[128]{0:T(128)S(1)}) all-reduce(f32[128]{0:T(128)S(1)} %get-tuple-element.403, f32[128]{0:T(128)S(1)} %get-tuple-element.401), channel_id=1, replica_groups=mesh['dp'=4,'seq'=64,'tensor'=2] {'dp','seq','tensor'}, use_global_device_ids=true, to_apply=%region_20.21 | all-reduce | flops 256 | bytes 2048 | tf_op jit(solution)/shard_map/psum | solution.py:129
  (146 shorter events, 35.1 us)
Async XLA Ops:
  0.6 28.4 %copy-start = (s32[1,64,3]{1,0,2:T(1,128)S(1)}, s32[1,64,3]{1,0,2:T(1,128)}, u32[]{:S(2)}) copy-start(s32[1,64,3]{1,0,2:T(1,128)} %param.22) | copy-start | bytes 2308
  0.6 1.4 copy-start.17
  2.5 20.2 %copy-start.9 = (f32[1,384,768]{1,2,0:T(8,128)}, f32[1,384,768]{1,2,0:T(8,128)S(1)}, u32[]{:S(2)}) copy-start(f32[1,384,768]{1,2,0:T(8,128)S(1)} %convert_element_type.161) | copy-start | bytes 3538948
  3.2 1.4 copy-start.19
  3.4 1.2 copy-start.13
  3.4 18.1 %copy-start.16 = (bf16[1,384,768]{2,1,0:T(8,128)(2,1)S(1)}, bf16[1,384,768]{2,1,0:T(8,128)(2,1)}, u32[]{:S(2)}) copy-start(bf16[1,384,768]{2,1,0:T(8,128)(2,1)} %param.16) | copy-start | bytes 1769476
  4.6 18.0 %copy-start.28 = (f32[128]{0:T(128)S(1)}, f32[128]{0:T(128)}, u32[]{:S(2)}) copy-start(f32[128]{0:T(128)} %param.20) | copy-start | bytes 1540
  4.6 30.6 %collective-permute-start = (bf16[2,384,6,128]{1,3,2,0:T(8,128)(2,1)}, bf16[2,384,6,128]{1,3,2,0:T(8,128)(2,1)}, u32[]{:S(2)}, u32[]{:S(2)}) collective-permute-start(bf16[2,384,6,128]{1,3,2,0:T(8,128)(2,1)} %pad_maximum_fusion), channel_id=1, source_target_pairs={{2,0},{4,2},{6,4},{8,6},{10,8},{12,10},{14,12},{16,14},{18,16},{20... | collective-permute-start | bytes 3538952 | tf_op jit(solution)/shard_map/ppermute | solution.py:16
  6.0 41.7 %collective-permute-start.1 = (bf16[2,384,6,128]{1,3,2,0:T(8,128)(2,1)}, bf16[2,384,6,128]{1,3,2,0:T(8,128)(2,1)}, u32[]{:S(2)}, u32[]{:S(2)}) collective-permute-start(bf16[2,384,6,128]{1,3,2,0:T(8,128)(2,1)} %pad_maximum_fusion), channel_id=1, source_target_pairs={{0,2},{2,4},{4,6},{6,8},{8,10},{10,12},{12,14},{14,16},{16,18},{18... | collective-permute-start | bytes 3538952 | tf_op jit(solution)/shard_map/ppermute | solution.py:16
  12.6 188.2 %collective-permute-start.2 = (bf16[2,384,6,128]{1,3,2,0:T(8,128)(2,1)}, bf16[2,384,6,128]{1,3,2,0:T(8,128)(2,1)}, u32[]{:S(2)}, u32[]{:S(2)}) collective-permute-start(bf16[2,384,6,128]{1,3,2,0:T(8,128)(2,1)} %pad_maximum_fusion), channel_id=1, source_target_pairs={{4,0},{6,2},{8,4},{10,6},{12,8},{14,10},{16,12},{18,14},{20,16},{2... | collective-permute-start | bytes 3538952 | tf_op jit(solution)/shard_map/ppermute | solution.py:16
  13.9 189.4 %collective-permute-start.3 = (bf16[2,384,6,128]{1,3,2,0:T(8,128)(2,1)}, bf16[2,384,6,128]{1,3,2,0:T(8,128)(2,1)}, u32[]{:S(2)}, u32[]{:S(2)}) collective-permute-start(bf16[2,384,6,128]{1,3,2,0:T(8,128)(2,1)} %pad_maximum_fusion), channel_id=1, source_target_pairs={{0,4},{2,6},{4,8},{6,10},{8,12},{10,14},{12,16},{14,18},{16,20},{1... | collective-permute-start | bytes 3538952 | tf_op jit(solution)/shard_map/ppermute | solution.py:16
  20.3 185.4 %collective-permute-start.4 = (bf16[2,384,6,128]{1,3,2,0:T(8,128)(2,1)}, bf16[2,384,6,128]{1,3,2,0:T(8,128)(2,1)}, u32[]{:S(2)}, u32[]{:S(2)}) collective-permute-start(bf16[2,384,6,128]{1,3,2,0:T(8,128)(2,1)} %pad_maximum_fusion), channel_id=1, source_target_pairs={{8,0},{10,2},{12,4},{14,6},{16,8},{18,10},{20,12},{22,14},{24,16},... | collective-permute-start | bytes 3538952 | tf_op jit(solution)/shard_map/ppermute | solution.py:16
  21.8 1.1 copy-start.7
  23.7 1.1 copy-start.14
  26.0 1.1 copy-start.18
  27.1 1.4 copy-start.32
  35.2 172.9 %collective-permute-start.5 = (bf16[2,384,6,128]{1,3,2,0:T(8,128)(2,1)}, bf16[2,384,6,128]{1,3,2,0:T(8,128)(2,1)S(1)}, u32[]{:S(2)}, u32[]{:S(2)}) collective-permute-start(bf16[2,384,6,128]{1,3,2,0:T(8,128)(2,1)} %pad_maximum_fusion), channel_id=1, source_target_pairs={{0,8},{2,10},{4,12},{6,14},{8,16},{10,18},{12,20},{14,22},{16,24},... | collective-permute-start | bytes 3538952 | tf_op jit(solution)/shard_map/ppermute | solution.py:16
  209.3 11.5 %copy-start.24 = (s32[7]{0:T(128)S(1)}, s32[7]{0:T(128)}, u32[]{:S(2)}) copy-start(s32[7]{0:T(128)} %constant.98.clone.14) | copy-start | bytes 88
  258.1 3.5 copy-start.2
  258.2 3.5 copy-start.30
  264.2 2.3 copy-start.4
  268.6 4.0 copy-start.5
  272.7 1.4 copy-start.33
  276.6 1.3 copy-start.3
  276.7 1.3 copy-start.31
  278.5 3.5 copy-start.2
  278.5 3.5 copy-start.30
  284.5 2.3 copy-start.4
  288.9 4.0 copy-start.5
  293.0 1.4 copy-start.33
  297.0 1.2 copy-start.3
  297.0 1.2 copy-start.31
  298.7 85.2 %copy-start.27 = (f32[128]{0:T(128)S(1)}, f32[128]{0:T(128)}, u32[]{:S(2)}) copy-start(f32[128]{0:T(128)} %param.21) | copy-start | bytes 1540
  298.7 85.2 %copy-start.6 = (f32[384,6,128]{0,2,1:T(8,128)S(1)}, f32[384,6,128]{0,2,1:T(8,128)}, u32[]{:S(2)}) copy-start(f32[384,6,128]{0,2,1:T(8,128)} %get-tuple-element.189) | copy-start | bytes 3538948
  298.7 85.1 %copy-start.8 = (f32[1,384,768]{1,2,0:T(8,128)S(1)}, f32[1,384,768]{1,2,0:T(8,128)}, u32[]{:S(2)}) copy-start(f32[1,384,768]{1,2,0:T(8,128)} %copy-done.7) | copy-start | bytes 3538948
  298.7 85.1 %copy-start.23 = (f32[384,6]{0,1:T(8,128)S(1)}, f32[384,6]{0,1:T(8,128)}, u32[]{:S(2)}) copy-start(f32[384,6]{0,1:T(8,128)} %copy-done.22) | copy-start | bytes 27652
  298.7 85.1 %copy-start.29 = (f32[128]{0:T(128)S(1)}, f32[128]{0:T(128)}, u32[]{:S(2)}) copy-start(f32[128]{0:T(128)} %param.20) | copy-start | bytes 1540
  304.3 54.7 %collective-permute-start.11 = (bf16[2,384,6,128]{1,3,2,0:T(8,128)(2,1)S(1)}, bf16[2,384,6,128]{1,3,2,0:T(8,128)(2,1)S(1)}, u32[]{:S(2)}, u32[]{:S(2)}) collective-permute-start(bf16[2,384,6,128]{1,3,2,0:T(8,128)(2,1)S(1)} %get-tuple-element.470), channel_id=1, source_target_pairs={{8,0},{10,2},{12,4},{14,6},{16,8},{18,10},{20,12},{22,14},{24,16},... | collective-permute-start | bytes 3538952 | tf_op jit(solution)/shard_map/ppermute | solution.py:16
  305.6 84.5 %collective-permute-start.10 = (bf16[2,384,6,128]{1,3,2,0:T(8,128)(2,1)}, bf16[2,384,6,128]{1,3,2,0:T(8,128)(2,1)}, u32[]{:S(2)}, u32[]{:S(2)}) collective-permute-start(bf16[2,384,6,128]{1,3,2,0:T(8,128)(2,1)} %get-tuple-element.466), channel_id=1, source_target_pairs={{0,8},{2,10},{4,12},{6,14},{8,16},{10,18},{12,20},{14,22},{16,24},... | collective-permute-start | bytes 3538952 | tf_op jit(solution)/shard_map/ppermute | solution.py:16
  314.5 155.6 %collective-permute-start.9 = (bf16[2,384,6,128]{1,3,2,0:T(8,128)(2,1)}, bf16[2,384,6,128]{1,3,2,0:T(8,128)(2,1)}, u32[]{:S(2)}, u32[]{:S(2)}) collective-permute-start(bf16[2,384,6,128]{1,3,2,0:T(8,128)(2,1)} %get-tuple-element.467), channel_id=1, source_target_pairs={{4,0},{6,2},{8,4},{10,6},{12,8},{14,10},{16,12},{18,14},{20,16},{2... | collective-permute-start | bytes 3538952 | tf_op jit(solution)/shard_map/ppermute | solution.py:16
  315.8 154.3 %collective-permute-start.8 = (bf16[2,384,6,128]{1,3,2,0:T(8,128)(2,1)}, bf16[2,384,6,128]{1,3,2,0:T(8,128)(2,1)}, u32[]{:S(2)}, u32[]{:S(2)}) collective-permute-start(bf16[2,384,6,128]{1,3,2,0:T(8,128)(2,1)} %get-tuple-element.468), channel_id=1, source_target_pairs={{0,4},{2,6},{4,8},{6,10},{8,12},{10,14},{12,16},{14,18},{16,20},{1... | collective-permute-start | bytes 3538952 | tf_op jit(solution)/shard_map/ppermute | solution.py:16
  321.7 190.3 %collective-permute-start.7 = (bf16[2,384,6,128]{1,3,2,0:T(8,128)(2,1)S(1)}, bf16[2,384,6,128]{1,3,2,0:T(8,128)(2,1)}, u32[]{:S(2)}, u32[]{:S(2)}) collective-permute-start(bf16[2,384,6,128]{1,3,2,0:T(8,128)(2,1)S(1)} %get-tuple-element.469), channel_id=1, source_target_pairs={{2,0},{4,2},{6,4},{8,6},{10,8},{12,10},{14,12},{16,14},{18,16},{20... | collective-permute-start | bytes 3538952 | tf_op jit(solution)/shard_map/ppermute | solution.py:16
  359.0 25.3 %copy-start.15 = (bf16[2,384,6,128]{1,3,2,0:T(8,128)(2,1)}, bf16[2,384,6,128]{1,3,2,0:T(8,128)(2,1)S(1)}, u32[]{:S(2)}) copy-start(bf16[2,384,6,128]{1,3,2,0:T(8,128)(2,1)S(1)} %collective-permute-done.11) | copy-start | bytes 3538948
  359.0 153.0 %collective-permute-start.6 = (bf16[2,384,6,128]{1,3,2,0:T(8,128)(2,1)S(1)}, bf16[2,384,6,128]{1,3,2,0:T(8,128)(2,1)}, u32[]{:S(2)}, u32[]{:S(2)}) collective-permute-start(bf16[2,384,6,128]{1,3,2,0:T(8,128)(2,1)S(1)} %get-tuple-element.465), channel_id=1, source_target_pairs={{0,2},{2,4},{4,6},{6,8},{8,10},{10,12},{12,14},{14,16},{16,18},{18... | collective-permute-start | bytes 3538952 | tf_op jit(solution)/shard_map/ppermute | solution.py:16
  516.8 1.3 copy-start.10
  516.8 1.3 copy-start.21
  518.4 1.1 copy-start.12
  519.4 173.1 %copy-start.1 = (s32[1,64,3]{1,0,2:T(1,128)S(1)}, s32[1,64,3]{1,0,2:T(1,128)}, u32[]{:S(2)}) copy-start(s32[1,64,3]{1,0,2:T(1,128)} %param.22) | copy-start | bytes 2308
  (5 other events, 4.1 us)
where the time goes:
time: 690 us; the launch traced here: 693 us
  waiting for transfers between devices  319 us (46%)
  blocking collectives  170 us (25%)
  starting transfers between devices  70.6 us (10%)
  local copies, waits for them, and re-layouts  56.1 us (8%)
  matrix products  36.3 us (5%)
  loops' own time  19.8 us (3%)
  other arithmetic  19.6 us (3%)
    ppermute x12, waiting for transfers between devices, shifted(): return lax.ppermute(block, axis, route)  319 us
    psum x1, blocking collectives, shards(): lax.psum((gain_part_q, gain_part_k), ('dp', 'seq', 'tensor'))  170 us
    ppermute x12, starting transfers between devices, shifted(): return lax.ppermute(block, axis, route)  70.6 us
    unnamed x68, local copies, waits for them, and re-layouts  35.1 us
  transfers between devices with their start and end apart: 12, of which 6 were waited for; matrix products, arithmetic and copies ran while one was open for 3% of the time, Pallas kernels for 0%

commit v1 on v0

v1 whole, which is shorter than its diff:
```python
import functools

import jax
import jax.numpy as jnp
from jax import lax
from jax.experimental import pallas as pl
from jax.experimental.pallas import tpu as pltpu
from jax.sharding import PartitionSpec as P

MESH = pl.DeviceIdType.MESH
EPS = 1e-06
LOG2E = 1.4426950408889634
FAR = 1e30
ROWS = 384
HD = 128
HEADS_HERE = 6
BLOCK = 128
RING = 8
NEAR = 4
F32 = jnp.float32
BF16 = jnp.bfloat16


def flip(z, mask):
    result = z
    for bit in (1, 2, 4):
        if mask & bit:
            result = result + bit - 2 * bit * ((z // bit) % 2)
    return result


def dot_t(a, b):
    return lax.dot_general(a, b, (((1,), (1,)), ((), ())), preferred_element_type=F32)


def dot(a, b):
    return lax.dot_general(a, b, (((1,), (0,)), ((), ())), preferred_element_type=F32)


def inverse_norm(wide):
    return lax.rsqrt(jnp.mean(wide * wide, axis=-1, keepdims=True) + EPS)


def stacked(rows):
    place = lax.broadcasted_iota(jnp.int32, (8, rows[0].shape[-1]), 0)
    out = jnp.broadcast_to(rows[-1], place.shape)
    for index in range(len(rows) - 2, -1, -1):
        out = jnp.where(place == index, rows[index], out)
    return out


def attention_kernel(
    lists, counts, q_ref, k_ref, v_ref, g_ref, gain_q_ref, gain_k_ref,
    dq_ref, dk_ref, dv_ref, gain_ref,
    slots, keys, key_t, part_out, part_in, final_out, final_in, dq32, dq_out, ret_in, ds_ref, dk_acc, dv_acc,
    slot_send, slot_recv, part_send, part_recv, final_send, final_recv, ret_send, ret_recv,
):
    factor = HD ** (-0.5)
    scale2 = factor * LOG2E
    mine = lax.axis_index("seq")
    y, z = mine // RING, mine % RING
    late = z // 4
    y_next = (y + 1 - 2 * late + RING) % RING
    y_prev = (y - 1 + 2 * late + RING) % RING
    along_w = y * RING + flip(z, 1)
    along_h = y * RING + flip(z, 2)
    relay = y * RING + flip(z, 6)
    along_t = y * RING + flip(z, 4)
    along_u = y_prev * RING + flip(z, 4)
    below = y_next * RING + z
    above = y_prev * RING + z
    owners = (along_w, along_h, along_t, along_u)

    barrier = pltpu.get_barrier_semaphore()
    for partner in (along_w, along_h, relay, along_t, along_u, below, above):
        pl.semaphore_signal(barrier, inc=1, device_id={"seq": partner}, device_id_type=MESH)

    def lanes(h):
        return pl.ds(pl.multiple_of(h * HD, HD), HD)

    def prepare_q(h, carry):
        wide = q_ref[:, lanes(h)].astype(F32)
        slots[0, h, 0] = (wide * inverse_norm(wide) * gain_q_ref[...]).astype(BF16)
        slots[0, h, 1] = g_ref[:, lanes(h)]
        return carry

    def prepare_k(h, carry):
        wide = k_ref[:, lanes(h)].astype(F32)
        key = (wide * inverse_norm(wide) * gain_k_ref[...]).astype(BF16)
        keys[h, 0] = key
        keys[h, 1] = v_ref[:, lanes(h)]
        key_t[h] = key.astype(F32).T.astype(BF16)
        return carry

    def remote(src, dst, send, recv, target):
        return pltpu.make_async_remote_copy(
            src_ref=src, dst_ref=dst, send_sem=send, recv_sem=recv, device_id={"seq": target}, device_id_type=MESH
        )

    def fetch(source, place, h, target):
        return remote(slots.at[source, h], slots.at[place, h], slot_send.at[place - 1, h], slot_recv.at[place - 1, h], target)

    def to_w(h):
        return fetch(0, 1, h, along_w)

    def to_h(h):
        return fetch(0, 2, h, along_h)

    def to_relay(h):
        return fetch(2, 3, h, relay)

    def to_y(h):
        return fetch(3, 4, h, below)

    def part_copy(place, h):
        return remote(
            part_out.at[place, h], part_in.at[place, h], part_send.at[place, h], part_recv.at[place, h], owners[place - 1]
        )

    def final_copy(place, h):
        return remote(
            final_out.at[place, h], final_in.at[place, h], final_send.at[place, h], final_recv.at[place, h], owners[place - 1]
        )

    def ret_copy(place, h, target):
        return remote(
            dq_out.at[place, h], ret_in.at[place, h], ret_send.at[place, h], ret_recv.at[place, h], target
        )

    def ret_w(h):
        return ret_copy(0, h, along_w)

    def ret_h(h):
        return ret_copy(1, h, along_h)

    def ret_relay(h):
        return ret_copy(2, h, relay)

    def ret_y(h):
        return ret_copy(3, h, above)

    flags = []
    for owner in owners:
        hit = jnp.int32(0)
        for entry in range(1, 3):
            same = jnp.where(lists[mine, entry] == owner, 1, 0)
            hit = hit + jnp.where(entry < counts[mine], same, 0)
        flags.append(hit > 0)

    def stats(place, h):
        query, grad = slots[place, h, 0], slots[place, h, 1]
        top = total = inner = None
        for block in range(ROWS // BLOCK):
            rows = pl.ds(block * BLOCK, BLOCK)
            scores = dot_t(keys[h, 0, rows], query) * scale2
            dprob = dot_t(keys[h, 1, rows], grad)
            high = jnp.max(scores, axis=0, keepdims=True)
            new_top = high if top is None else jnp.maximum(top, high)
            weight = jnp.exp2(scores - new_top)
            new_total = jnp.sum(weight, axis=0, keepdims=True)
            new_inner = jnp.sum(weight * dprob, axis=0, keepdims=True)
            if top is not None:
                keep = jnp.exp2(top - new_top)
                new_total = new_total + total * keep
                new_inner = new_inner + inner * keep
            top, total, inner = new_top, new_total, new_inner
        part_out[place, h] = stacked((top, total, inner))

    def combine(h):
        parts = [part_out[0, h]] + [part_in[n + 1, h] for n in range(NEAR)]
        tops = [parts[0][0:1]] + [jnp.where(flags[n], parts[n + 1][0:1], -FAR) for n in range(NEAR)]
        top = functools.reduce(jnp.maximum, tops)
        weights = [jnp.exp2(t - top) for t in tops]
        total = sum(p[1:2] * w for p, w in zip(parts, weights))
        inner = sum(p[2:3] * w for p, w in zip(parts, weights))
        log_total = top + jnp.log(total) * LOG2E
        delta = inner / total
        final_in[0, h] = stacked((log_total, delta))
        for n in range(NEAR):
            final_out[n + 1, h] = stacked((jnp.where(flags[n], log_total, FAR), delta))

    def grads(place, h):
        query, grad = slots[place, h, 0], slots[place, h, 1]
        final = final_in[place, h]
        log_total, delta = final[0:1], final[1:2]
        for block in range(ROWS // BLOCK):
            rows = pl.ds(block * BLOCK, BLOCK)
            scores = dot_t(keys[h, 0, rows], query) * scale2
            dprob = dot_t(keys[h, 1, rows], grad)
            prob = jnp.exp2(scores - log_total)
            dscore = (prob * (dprob - delta)).astype(BF16)
            ds_ref[rows] = dscore
            dv_acc[rows] += dot(prob.astype(BF16), grad)
            dk_acc[rows] += dot(dscore, query)
        dq32[place, h] = dot(key_t[h], ds_ref[...]) * factor

    def norm_backward(grad, raw, gain):
        wide = raw.astype(F32)
        inverse = inverse_norm(wide)
        normed = wide * inverse
        scaled = grad * gain
        mean = jnp.mean(normed * scaled, axis=-1, keepdims=True)
        return ((scaled - normed * mean) * inverse).astype(BF16), jnp.sum(grad * normed, axis=0, keepdims=True)

    def backward(h):
        dk_acc[...] = jnp.zeros_like(dk_acc)
        dv_acc[...] = jnp.zeros_like(dv_acc)
        lax.fori_loop(0, NEAR + 1, lambda place, carry: (grads(place, h), carry)[1], 0)
        dq_out[0, h] = dq32[1, h].astype(BF16)
        dq_out[3, h] = dq32[4, h].astype(BF16)

    def finish_k(h):
        dv_ref[:, lanes(h)] = dv_acc[...].astype(BF16)
        grad, gain = norm_backward(dk_acc[...] * factor, k_ref[:, lanes(h)], gain_k_ref[...])
        dk_ref[:, lanes(h)] = grad
        gain_ref[1:2] += gain

    def finish_q(h):
        total = dq32[0, h] + ret_in[0, h].astype(F32) + ret_in[1, h].astype(F32)
        grad, gain = norm_backward(total.T, q_ref[:, lanes(h)], gain_q_ref[...])
        dq_ref[:, lanes(h)] = grad
        gain_ref[0:1] += gain

    gain_ref[...] = jnp.zeros_like(gain_ref)
    lax.fori_loop(0, HEADS_HERE, prepare_q, 0)
    pl.semaphore_wait(barrier, 7)
    to_h(0).start()
    to_h(1).start()
    to_w(0).start()
    lax.fori_loop(0, HEADS_HERE, prepare_k, 0)

    def step(i, carry):
        def on(lag, stage):
            h = i - lag

            @pl.when(jnp.logical_and(h >= 0, h < HEADS_HERE))
            def _():
                stage(h)

        def arrive(h):
            to_h(h).wait_recv()
            to_relay(h).start()

            @pl.when(h + 2 < HEADS_HERE)
            def _():
                to_h(h + 2).start()

            @pl.when(h + 1 < HEADS_HERE)
            def _():
                to_w(h + 1).start()

            stats(0, h)
            stats(2, h)

        def pass_on(h):
            to_relay(h).wait_recv()
            to_y(h).start()

        def near_w(h):
            to_w(h).wait_recv()
            stats(1, h)

        def send_parts(h):
            to_y(h).wait_recv()
            stats(4, h)
            for place in range(1, NEAR + 1):
                part_copy(place, h).start()

        def pairs(h):
            for place in range(1, NEAR + 1):
                final_copy(place, h).wait_recv()
            backward(h)
            ret_w(h).start()
            ret_y(h).start()
            finish_k(h)

        def send_finals(h):
            for place in range(1, NEAR + 1):
                part_copy(place, h).wait_recv()
            combine(h)
            for place in range(1, NEAR + 1):
                final_copy(place, h).start()

        def back_y(h):
            ret_y(h).wait_recv()
            dq_out[2, h] = (dq32[3, h] + ret_in[3, h].astype(F32)).astype(BF16)
            ret_relay(h).start()

        def back_relay(h):
            ret_relay(h).wait_recv()
            dq_out[1, h] = (dq32[2, h] + ret_in[2, h].astype(F32)).astype(BF16)
            ret_h(h).start()

        def back_home(h):
            ret_w(h).wait_recv()
            ret_h(h).wait_recv()
            finish_q(h)

        on(0, arrive)
        on(1, pass_on)
        on(0, near_w)
        on(1, lambda h: stats(3, h))
        on(2, send_parts)
        on(3, pairs)
        on(2, send_finals)
        on(4, back_y)
        on(5, back_relay)
        on(6, back_home)
        return carry

    lax.fori_loop(0, HEADS_HERE + 6, step, 0)

    def drain(h, carry):
        for copy in (to_w, to_h, to_relay, to_y, ret_w, ret_h, ret_relay, ret_y):
            copy(h).wait_send()
        for place in range(1, NEAR + 1):
            part_copy(place, h).wait_send()
            final_copy(place, h).wait_send()
        return carry

    lax.fori_loop(0, HEADS_HERE, drain, 0)


def attention(lists, counts, q, k, v, g, gain_q, gain_k):
    n = HEADS_HERE
    vmem = pl.BlockSpec(memory_space=pltpu.VMEM)
    smem = pl.BlockSpec(memory_space=pltpu.SMEM)
    big = jax.ShapeDtypeStruct((ROWS, n * HD), BF16)
    sem = pltpu.SemaphoreType.DMA
    return pl.pallas_call(
        attention_kernel,
        name="tile_attention",
        out_shape=(big, big, big, jax.ShapeDtypeStruct((8, HD), F32)),
        in_specs=[smem, smem] + [vmem] * 6,
        out_specs=(vmem,) * 4,
        scratch_shapes=[
            pltpu.VMEM((5, n, 2, ROWS, HD), BF16),
            pltpu.VMEM((n, 2, ROWS, HD), BF16),
            pltpu.VMEM((n, HD, ROWS), BF16),
            pltpu.VMEM((5, n, 8, ROWS), F32),
            pltpu.VMEM((5, n, 8, ROWS), F32),
            pltpu.VMEM((5, n, 8, ROWS), F32),
            pltpu.VMEM((5, n, 8, ROWS), F32),
            pltpu.VMEM((5, n, HD, ROWS), F32),
            pltpu.VMEM((4, n, HD, ROWS), BF16),
            pltpu.VMEM((4, n, HD, ROWS), BF16),
            pltpu.VMEM((ROWS, ROWS), BF16),
            pltpu.VMEM((ROWS, HD), F32),
            pltpu.VMEM((ROWS, HD), F32),
            sem((4, n)), sem((4, n)), sem((5, n)), sem((5, n)), sem((5, n)), sem((5, n)), sem((4, n)), sem((4, n)),
        ],
        compiler_params=pltpu.CompilerParams(collective_id=1, has_side_effects=True, vmem_limit_bytes=56 * 2**20),
    )(lists, counts, q, k, v, g, gain_q, gain_k)


def total_kernel(part_ref, out_ref, held_a, held_b, held_c, sends, recvs):
    x, s, c = lax.axis_index("dp"), lax.axis_index("seq"), lax.axis_index("tensor")
    y, z = s // RING, s % RING
    groups = (
        (held_a, x * 2 + c, lambda p: {"dp": p // 2, "tensor": p % 2}),
        (held_b, y, lambda p: {"seq": p * RING + z}),
        (held_c, z, lambda p: {"seq": y * RING + p}),
    )
    barrier = pltpu.get_barrier_semaphore()
    for _, me, where in groups:
        for step in range(1, 8):
            pl.semaphore_signal(barrier, inc=1, device_id=where((me + step) % 8), device_id_type=MESH)
    value = part_ref[...]
    pl.semaphore_wait(barrier, 21)
    for g, (held, me, where) in enumerate(groups):
        held[me] = value

        def copy(step):
            return pltpu.make_async_remote_copy(
                src_ref=held.at[me], dst_ref=held.at[me], send_sem=sends.at[g, step], recv_sem=recvs.at[g, step],
                device_id=where((me + step) % 8), device_id_type=MESH,
            )

        copies = [copy(step) for step in range(1, 8)]
        for item in copies:
            item.start()
        for item in copies:
            item.wait_recv()
        for item in copies:
            item.wait_send()
        value = held[0]
        for place in range(1, 8):
            value = value + held[place]
    out_ref[...] = value


def total(part):
    vmem = pl.BlockSpec(memory_space=pltpu.VMEM)
    sem = pltpu.SemaphoreType.DMA
    return pl.pallas_call(
        total_kernel,
        name="gain_total",
        out_shape=jax.ShapeDtypeStruct((8, HD), F32),
        in_specs=[vmem],
        out_specs=vmem,
        scratch_shapes=[pltpu.VMEM((8, 8, HD), F32)] * 3 + [sem((3, 8)), sem((3, 8))],
        compiler_params=pltpu.CompilerParams(collective_id=2, has_side_effects=True),
    )(part)


def shards(q_raw, k_raw, values, d_out, gain_q, gain_k, tile_lists, tile_counts):
    grad_q, grad_k, grad_v, gains = attention(
        tile_lists[0], tile_counts[0], q_raw[0], k_raw[0], values[0], d_out[0], gain_q[None], gain_k[None]
    )
    gains = total(gains)
    scale_back = (lax.axis_size("dp") * lax.axis_size("seq") * ROWS) ** (-0.5)
    return (grad_q[None], grad_k[None], grad_v[None], gains[0] * scale_back, gains[1] * scale_back)


def solution(mesh):
    split = P("dp", "seq", "tensor")
    return jax.shard_map(
        shards,
        mesh=mesh,
        in_specs=(split, split, split, split, P(), P(), P("dp", None, None), P("dp", None)),
        out_specs=(split, split, split, P(), P()),
        check_vma=False,
    )
```

time: 690 us -> 204 us (0.30)
  waiting for transfers between devices: 319 us -> 0 us
  Pallas kernels: 0 us -> 196 us
  blocking collectives: 170 us -> 0 us
  starting transfers between devices: 70.6 us -> 0 us
  local copies, waits for them, and re-layouts: 56.1 us -> 5.46 us
  matrix products: 36.3 us -> 0 us
  loops' own time: 19.8 us -> 0 us
  other arithmetic: 19.6 us -> 1.27 us
    ppermute x12 -> x0, waiting for transfers between devices: 319 us -> none  [shifted(): return lax.ppermute(block, axis, route)]
    pallas_call x0 -> x2, Pallas kernels: none -> 196 us  [the longest x1 168 us: attention(): pl.pallas_call(attention_kernel, name='tile_attention', out_shape=(big, b...]
    psum x1 -> x0, blocking collectives: 170 us -> none  [shards(): lax.psum((gain_part_q, gain_part_k), ('dp', 'seq', 'tensor'))]
    ppermute x12 -> x0, starting transfers between devices: 70.6 us -> none  [shifted(): return lax.ppermute(block, axis, route)]
    dot_general x16 -> x0, matrix products: 36.3 us -> none  [the longest x6 13.3 us: tile_scores(): jnp.einsum('qhd,khd->hqk', query, key_tile, preferred_element_type=jnp.fl...]
    unnamed x68 -> x8, local copies, waits for them, and re-layouts: 35.1 us -> 5.46 us
    another operation x3 -> x0, loops' own time: 19.8 us -> none  [the longest x1 11.3 us: shards(): lax.fori_loop(0, my_count, backward_pass, (zero_q, empty_terms))]
    reduce_sum x13 -> x0, other arithmetic: 10 us -> none  [the longest x5 6.63 us: pair_of(): slot = jnp.sum(jnp.where(target_ids == target, slot_ids, 0))]
  transfers between devices with their start and end apart: 12 -> 0, of which waited for: 6 -> 0; matrix products, arithmetic and copies ran while one was open for 3% -> 0% of each run, Pallas kernels for 0% -> 0%
where the time goes in v1:
time: 204 us; the launch traced here: 203 us
  Pallas kernels  196 us (96%)
  local copies, waits for them, and re-layouts  5.46 us (3%)
    pallas_call x1, Pallas kernels, attention(): pl.pallas_call(attention_kernel, name='tile_attention', out_shape=(big, b...  168 us
    pallas_call x1, Pallas kernels, total(): pl.pallas_call(total_kernel, name='gain_total', out_shape=jax.ShapeDtypeS...  27.7 us
    unnamed x8, local copies, waits for them, and re-layouts  5.46 us

profile of v1, /device:TPU:1, one launch (start us, length us, event | category | flops | bytes accessed | tf_op | source)
XLA Modules:
  0.0 203.4 jit_solution(287460494538483470)
XLA Ops:
  0.6 1.4 copy.13
  2.0 168.3 %tile_attention.1 = (bf16[384,768]{1,0:T(8,128)(2,1)}, bf16[384,768]{1,0:T(8,128)(2,1)}, bf16[384,768]{1,0:T(8,128)(2,1)}, f32[8,128]{1,0:T(8,128)}) custom-call(s32[64,3]{1,0:T(8,128)} %bitcast.22, s32[64]{0:T(128)} %bitcast.23, bf16[384,768]{1,0:T(8,128)(2,1)} %bitcast.15, bf16[384,768]{1,0:T(8,128)(2,1)} %bitcast.16, bf16[384,768]{1,0:T(8,128)(2,1)} %bitcast.17, ...), custom_call_target="tpu_custom_call" | custom-call | tf_op jit(solution)/shard_map/tile_attention/pallas_call | solution.py:330
  170.3 27.7 %gain_total.1 = f32[8,128]{1,0:T(8,128)} custom-call(f32[8,128]{1,0:T(8,128)} %get-tuple-element.12.part_ref), custom_call_target="tpu_custom_call" | custom-call | tf_op jit(solution)/shard_map/gain_total/pallas_call | solution.py:395
  198.0 1.3 multiply_bitcast_fusion
  199.3 0.0 copy-start.1
  199.3 2.0 copy.17
  201.3 0.0 copy-done.1
  201.3 0.0 copy-start
  201.3 0.8 copy.18
  202.1 0.5 copy-done
  202.5 0.8 copy.19
Async XLA Ops:
  199.3 2.0 copy-start.1
  201.3 1.3 copy-start

commit v2 on v1

--- a/solution.py
+++ b/solution.py
@@ -41,19 +41,17 @@
     return lax.rsqrt(jnp.mean(wide * wide, axis=-1, keepdims=True) + EPS)
 
 
-def stacked(rows):
-    place = lax.broadcasted_iota(jnp.int32, (8, rows[0].shape[-1]), 0)
-    out = jnp.broadcast_to(rows[-1], place.shape)
-    for index in range(len(rows) - 2, -1, -1):
-        out = jnp.where(place == index, rows[index], out)
-    return out
+def stacked(first, second):
+    place = lax.broadcasted_iota(jnp.int32, (2, first.shape[-1]), 0)
+    return jnp.where(place == 0, first, second)
 
 
 def attention_kernel(
     lists, counts, q_ref, k_ref, v_ref, g_ref, gain_q_ref, gain_k_ref,
-    dq_ref, dk_ref, dv_ref, gain_ref,
+    dq_ref, dk_ref, dv_ref, gain_out_ref,
     slots, keys, key_t, part_out, part_in, final_out, final_in, dq32, dq_out, ret_in, ds_ref, dk_acc, dv_acc,
-    slot_send, slot_recv, part_send, part_recv, final_send, final_recv, ret_send, ret_recv,
+    gain_ref, gain_a, gain_b, gain_c,
+    slot_send, slot_recv, part_send, part_recv, final_send, final_recv, ret_send, ret_recv, gain_send, gain_recv,
 ):
     factor = HD ** (-0.5)
     scale2 = factor * LOG2E
@@ -74,6 +72,15 @@
     barrier = pltpu.get_barrier_semaphore()
     for partner in (along_w, along_h, relay, along_t, along_u, below, above):
         pl.semaphore_signal(barrier, inc=1, device_id={"seq": partner}, device_id_type=MESH)
+    clip, core = lax.axis_index("dp"), lax.axis_index("tensor")
+    groups = (
+        (gain_a, clip * 2 + core, lambda p: {"dp": p // 2, "tensor": p % 2}),
+        (gain_b, y, lambda p: {"seq": p * RING + z}),
+        (gain_c, z, lambda p: {"seq": y * RING + p}),
+    )
+    for _, me, where in groups:
+        for hop in range(1, RING):
+            pl.semaphore_signal(barrier, inc=1, device_id=where((me + hop) % RING), device_id_type=MESH)
 
     def lanes(h):
         return pl.ds(pl.multiple_of(h * HD, HD), HD)
@@ -164,20 +171,19 @@
                 new_total = new_total + total * keep
                 new_inner = new_inner + inner * keep
             top, total, inner = new_top, new_total, new_inner
-        part_out[place, h] = stacked((top, total, inner))
+        part_out[place, h] = stacked(top + jnp.log(total) * LOG2E, inner / total)
 
     def combine(h):
         parts = [part_out[0, h]] + [part_in[n + 1, h] for n in range(NEAR)]
         tops = [parts[0][0:1]] + [jnp.where(flags[n], parts[n + 1][0:1], -FAR) for n in range(NEAR)]
         top = functools.reduce(jnp.maximum, tops)
         weights = [jnp.exp2(t - top) for t in tops]
-        total = sum(p[1:2] * w for p, w in zip(parts, weights))
-        inner = sum(p[2:3] * w for p, w in zip(parts, weights))
+        total = sum(weights)
         log_total = top + jnp.log(total) * LOG2E
-        delta = inner / total
-        final_in[0, h] = stacked((log_total, delta))
+        delta = sum(p[1:2] * w for p, w in zip(parts, weights)) / total
+        final_in[0, h] = stacked(log_total, delta)
         for n in range(NEAR):
-            final_out[n + 1, h] = stacked((jnp.where(flags[n], log_total, FAR), delta))
+            final_out[n + 1, h] = stacked(jnp.where(flags[n], log_total, FAR), delta)
 
     def grads(place, h):
         query, grad = slots[place, h, 0], slots[place, h, 1]
@@ -211,23 +217,52 @@
 
     def finish_k(h):
         dv_ref[:, lanes(h)] = dv_acc[...].astype(BF16)
-        grad, gain = norm_backward(dk_acc[...] * factor, k_ref[:, lanes(h)], gain_k_ref[...])
+        grad_key = dk_acc[...] * factor
+        grad, gain = norm_backward(grad_key, k_ref[:, lanes(h)], gain_k_ref[...])
         dk_ref[:, lanes(h)] = grad
-        gain_ref[1:2] += gain
+        paired = jnp.sum(grad_key * keys[h, 0].astype(F32), axis=0, keepdims=True) / gain_q_ref[...]
+        gain_ref[...] += stacked(paired, gain)
 
     def finish_q(h):
         total = dq32[0, h] + ret_in[0, h].astype(F32) + ret_in[1, h].astype(F32)
-        grad, gain = norm_backward(total.T, q_ref[:, lanes(h)], gain_q_ref[...])
+        grad, _ = norm_backward(total.T, q_ref[:, lanes(h)], gain_q_ref[...])
         dq_ref[:, lanes(h)] = grad
-        gain_ref[0:1] += gain
+
+    def gain_copies(g):
+        held, me, where = groups[g]
+        return [
+            pltpu.make_async_remote_copy(
+                src_ref=held.at[me], dst_ref=held.at[me], send_sem=gain_send.at[g, hop], recv_sem=gain_recv.at[g, hop],
+                device_id=where((me + hop) % RING), device_id_type=MESH,
+            )
+            for hop in range(1, RING)
+        ]
+
+    def gain_start(g, value):
+        held, me, _ = groups[g]
+        held[me] = value
+        for copy in gain_copies(g):
+            copy.start()
+
+    def gain_finish(g):
+        held, _, _ = groups[g]
+        for copy in gain_copies(g):
+            copy.wait_recv()
+        value = held[0]
+        for place in range(1, RING):
+            value = value + held[place]
+        return value
 
     gain_ref[...] = jnp.zeros_like(gain_ref)
     lax.fori_loop(0, HEADS_HERE, prepare_q, 0)
-    pl.semaphore_wait(barrier, 7)
+    pl.semaphore_wait(barrier, 7 + 3 * (RING - 1))
     to_h(0).start()
+    to_w(0).start()
     to_h(1).start()
-    to_w(0).start()
+    to_h(2).start()
     lax.fori_loop(0, HEADS_HERE, prepare_k, 0)
+
+    last = HEADS_HERE + 3
 
     def step(i, carry):
         def on(lag, stage):
@@ -241,9 +276,9 @@
             to_h(h).wait_recv()
             to_relay(h).start()
 
-            @pl.when(h + 2 < HEADS_HERE)
+            @pl.when(h + 3 < HEADS_HERE)
             def _():
-                to_h(h + 2).start()
+                to_h(h + 3).start()
 
             @pl.when(h + 1 < HEADS_HERE)
             def _():
@@ -301,14 +336,18 @@
         on(0, near_w)
         on(1, lambda h: stats(3, h))
         on(2, send_parts)
-        on(3, pairs)
-        on(2, send_finals)
-        on(4, back_y)
-        on(5, back_relay)
-        on(6, back_home)
+        on(3, send_finals)
+        on(4, pairs)
+        pl.when(i == last)(lambda: gain_start(0, gain_ref[...]))
+        on(5, back_y)
+        on(6, back_relay)
+        on(7, back_home)
+        pl.when(i == last + 1)(lambda: gain_start(1, gain_finish(0)))
+        pl.when(i == last + 2)(lambda: gain_start(2, gain_finish(1)))
         return carry
 
-    lax.fori_loop(0, HEADS_HERE + 6, step, 0)
+    lax.fori_loop(0, HEADS_HERE + 7, step, 0)
+    gain_out_ref[...] = gain_finish(2) * (4 * 64 * ROWS) ** (-0.5)
 
     def drain(h, carry):
         for copy in (to_w, to_h, to_relay, to_y, ret_w, ret_h, ret_relay, ret_y):
@@ -319,6 +358,9 @@
         return carry
 
     lax.fori_loop(0, HEADS_HERE, drain, 0)
+    for g in range(3):
+        for copy in gain_copies(g):
+            copy.wait_send()
 
 
 def attention(lists, counts, q, k, v, g, gain_q, gain_k):
@@ -330,86 +372,39 @@
     return pl.pallas_call(
         attention_kernel,
         name="tile_attention",
-        out_shape=(big, big, big, jax.ShapeDtypeStruct((8, HD), F32)),
+        out_shape=(big, big, big, jax.ShapeDtypeStruct((2, HD), F32)),
         in_specs=[smem, smem] + [vmem] * 6,
         out_specs=(vmem,) * 4,
         scratch_shapes=[
             pltpu.VMEM((5, n, 2, ROWS, HD), BF16),
             pltpu.VMEM((n, 2, ROWS, HD), BF16),
             pltpu.VMEM((n, HD, ROWS), BF16),
-            pltpu.VMEM((5, n, 8, ROWS), F32),
-            pltpu.VMEM((5, n, 8, ROWS), F32),
-            pltpu.VMEM((5, n, 8, ROWS), F32),
-            pltpu.VMEM((5, n, 8, ROWS), F32),
+            pltpu.VMEM((5, n, 2, ROWS), F32),
+            pltpu.VMEM((5, n, 2, ROWS), F32),
+            pltpu.VMEM((5, n, 2, ROWS), F32),
+            pltpu.VMEM((5, n, 2, ROWS), F32),
             pltpu.VMEM((5, n, HD, ROWS), F32),
             pltpu.VMEM((4, n, HD, ROWS), BF16),
             pltpu.VMEM((4, n, HD, ROWS), BF16),
             pltpu.VMEM((ROWS, ROWS), BF16),
             pltpu.VMEM((ROWS, HD), F32),
             pltpu.VMEM((ROWS, HD), F32),
+            pltpu.VMEM((2, HD), F32),
+            pltpu.VMEM((RING, 2, HD), F32),
+            pltpu.VMEM((RING, 2, HD), F32),
+            pltpu.VMEM((RING, 2, HD), F32),
             sem((4, n)), sem((4, n)), sem((5, n)), sem((5, n)), sem((5, n)), sem((5, n)), sem((4, n)), sem((4, n)),
+            sem((3, RING)), sem((3, RING)),
         ],
         compiler_params=pltpu.CompilerParams(collective_id=1, has_side_effects=True, vmem_limit_bytes=56 * 2**20),
     )(lists, counts, q, k, v, g, gain_q, gain_k)
-
-
-def total_kernel(part_ref, out_ref, held_a, held_b, held_c, sends, recvs):
-    x, s, c = lax.axis_index("dp"), lax.axis_index("seq"), lax.axis_index("tensor")
-    y, z = s // RING, s % RING
-    groups = (
-        (held_a, x * 2 + c, lambda p: {"dp": p // 2, "tensor": p % 2}),
-        (held_b, y, lambda p: {"seq": p * RING + z}),
-        (held_c, z, lambda p: {"seq": y * RING + p}),
-    )
-    barrier = pltpu.get_barrier_semaphore()
-    for _, me, where in groups:
-        for step in range(1, 8):
-            pl.semaphore_signal(barrier, inc=1, device_id=where((me + step) % 8), device_id_type=MESH)
-    value = part_ref[...]
-    pl.semaphore_wait(barrier, 21)
-    for g, (held, me, where) in enumerate(groups):
-        held[me] = value
-
-        def copy(step):
-            return pltpu.make_async_remote_copy(
-                src_ref=held.at[me], dst_ref=held.at[me], send_sem=sends.at[g, step], recv_sem=recvs.at[g, step],
-                device_id=where((me + step) % 8), device_id_type=MESH,
-            )
-
-        copies = [copy(step) for step in range(1, 8)]
-        for item in copies:
-            item.start()
-        for item in copies:
-            item.wait_recv()
-        for item in copies:
-            item.wait_send()
-        value = held[0]
-        for place in range(1, 8):
-            value = value + held[place]
-    out_ref[...] = value
-
-
-def total(part):
-    vmem = pl.BlockSpec(memory_space=pltpu.VMEM)
-    sem = pltpu.SemaphoreType.DMA
-    return pl.pallas_call(
-        total_kernel,
-        name="gain_total",
-        out_shape=jax.ShapeDtypeStruct((8, HD), F32),
-        in_specs=[vmem],
-        out_specs=vmem,
-        scratch_shapes=[pltpu.VMEM((8, 8, HD), F32)] * 3 + [sem((3, 8)), sem((3, 8))],
-        compiler_params=pltpu.CompilerParams(collective_id=2, has_side_effects=True),
-    )(part)
 
 
 def shards(q_raw, k_raw, values, d_out, gain_q, gain_k, tile_lists, tile_counts):
     grad_q, grad_k, grad_v, gains = attention(
         tile_lists[0], tile_counts[0], q_raw[0], k_raw[0], values[0], d_out[0], gain_q[None], gain_k[None]
     )
-    gains = total(gains)
-    scale_back = (lax.axis_size("dp") * lax.axis_size("seq") * ROWS) ** (-0.5)
-    return (grad_q[None], grad_k[None], grad_v[None], gains[0] * scale_back, gains[1] * scale_back)
+    return (grad_q[None], grad_k[None], grad_v[None], gains[0], gains[1])
 
 
 def solution(mesh):

time: 204 us -> 160 us (0.78)
  Pallas kernels: 196 us -> 152 us
    pallas_call x1 -> x0, Pallas kernels: 27.7 us -> none  [total(): pl.pallas_call(total_kernel, name='gain_total', out_shape=jax.ShapeDtypeS...]
    pallas_call x1, Pallas kernels: 168 us -> 152 us  [attention(): pl.pallas_call(attention_kernel, name='tile_attention', out_shape=(big, b...]
    unnamed x8 -> x12, local copies, waits for them, and re-layouts: 5.46 us -> 6.13 us
where the time goes in v2:
time: 160 us; the launch traced here: 159 us
  Pallas kernels  152 us (95%)
  local copies, waits for them, and re-layouts  6.64 us (4%)
    pallas_call x1, Pallas kernels, attention(): pl.pallas_call(attention_kernel, name='tile_attention', out_shape=(big, b...  152 us
    unnamed x12, local copies, waits for them, and re-layouts  6.13 us

profile of v2, /device:TPU:1, one launch (start us, length us, event | category | flops | bytes accessed | tf_op | source)
XLA Modules:
  0.0 159.3 jit_solution(2640017316547106978)
XLA Ops:
  0.6 0.0 copy-start.2
  0.6 0.7 copy-done.2
  1.3 0.7 copy.13
  2.0 152.0 %tile_attention.1 = (bf16[384,768]{1,0:T(8,128)(2,1)}, bf16[384,768]{1,0:T(8,128)(2,1)}, bf16[384,768]{1,0:T(8,128)(2,1)}, f32[2,128]{1,0:T(2,128)}) custom-call(s32[64,3]{1,0:T(8,128)} %bitcast.22, s32[64]{0:T(128)} %bitcast.23, bf16[384,768]{1,0:T(8,128)(2,1)} %bitcast.15, bf16[384,768]{1,0:T(8,128)(2,1)} %bitcast.16, bf16[384,768]{1,0:T(8,128)(2,1)} %bitcast.17, ...), custom_call_target="tpu_custom_call" | custom-call | tf_op jit(solution)/shard_map/tile_attention/pallas_call | solution.py:372
  154.0 0.0 copy-start.3
  154.0 0.7 copy-done.3
  154.7 0.5 slice_bitcast_fusion
  155.2 0.0 copy-start.1
  155.2 2.0 %copy.17 = bf16[1,384,768]{2,1,0:T(8,128)(2,1)} copy(bf16[1,384,768]{2,1,0:T(8,128)(2,1)} %bitcast.21) | data formatting | bytes 1179648
  157.2 0.0 copy-done.1
  157.2 0.0 copy-start
  157.2 0.8 copy.18
  158.0 0.5 copy-done
  158.5 0.8 copy.19
Async XLA Ops:
  0.6 0.7 copy-start.2
  154.0 0.7 copy-start.3
  155.2 2.0 %copy-start.1 = (bf16[384,768]{1,0:T(8,128)(2,1)S(1)}, bf16[384,768]{1,0:T(8,128)(2,1)}, u32[]{:S(2)}) copy-start(bf16[384,768]{1,0:T(8,128)(2,1)} %get-tuple-element.10) | copy-start | bytes 1769476
  157.2 1.3 copy-start

commit v3 on v2

--- a/solution.py
+++ b/solution.py
@@ -48,7 +48,7 @@
 
 def attention_kernel(
     lists, counts, q_ref, k_ref, v_ref, g_ref, gain_q_ref, gain_k_ref,
-    dq_ref, dk_ref, dv_ref, gain_out_ref,
+    grads_ref, gain_q_out, gain_k_out,
     slots, keys, key_t, part_out, part_in, final_out, final_in, dq32, dq_out, ret_in, ds_ref, dk_acc, dv_acc,
     gain_ref, gain_a, gain_b, gain_c,
     slot_send, slot_recv, part_send, part_recv, final_send, final_recv, ret_send, ret_recv, gain_send, gain_recv,
@@ -150,7 +150,7 @@
     for owner in owners:
         hit = jnp.int32(0)
         for entry in range(1, 3):
-            same = jnp.where(lists[mine, entry] == owner, 1, 0)
+            same = jnp.where(lists[entry, 0, mine] == owner, 1, 0)
             hit = hit + jnp.where(entry < counts[mine], same, 0)
         flags.append(hit > 0)
 
@@ -211,22 +211,37 @@
     def backward(h):
         dk_acc[...] = jnp.zeros_like(dk_acc)
         dv_acc[...] = jnp.zeros_like(dv_acc)
-        lax.fori_loop(0, NEAR + 1, lambda place, carry: (grads(place, h), carry)[1], 0)
-        dq_out[0, h] = dq32[1, h].astype(BF16)
-        dq_out[3, h] = dq32[4, h].astype(BF16)
+
+        def one(index, carry):
+            place = NEAR - index
+            grads(place, h)
+
+            @pl.when(place == 4)
+            def _():
+                dq_out[3, h] = dq32[4, h].astype(BF16)
+                ret_y(h).start()
+
+            @pl.when(place == 1)
+            def _():
+                dq_out[0, h] = dq32[1, h].astype(BF16)
+                ret_w(h).start()
+
+            return carry
+
+        lax.fori_loop(0, NEAR + 1, one, 0)
 
     def finish_k(h):
-        dv_ref[:, lanes(h)] = dv_acc[...].astype(BF16)
+        grads_ref[2, :, lanes(h)] = dv_acc[...].astype(BF16)
         grad_key = dk_acc[...] * factor
         grad, gain = norm_backward(grad_key, k_ref[:, lanes(h)], gain_k_ref[...])
-        dk_ref[:, lanes(h)] = grad
+        grads_ref[1, :, lanes(h)] = grad
         paired = jnp.sum(grad_key * keys[h, 0].astype(F32), axis=0, keepdims=True) / gain_q_ref[...]
         gain_ref[...] += stacked(paired, gain)
 
     def finish_q(h):
         total = dq32[0, h] + ret_in[0, h].astype(F32) + ret_in[1, h].astype(F32)
         grad, _ = norm_backward(total.T, q_ref[:, lanes(h)], gain_q_ref[...])
-        dq_ref[:, lanes(h)] = grad
+        grads_ref[0, :, lanes(h)] = grad
 
     def gain_copies(g):
         held, me, where = groups[g]
@@ -305,8 +320,6 @@
             for place in range(1, NEAR + 1):
                 final_copy(place, h).wait_recv()
             backward(h)
-            ret_w(h).start()
-            ret_y(h).start()
             finish_k(h)
 
         def send_finals(h):
@@ -335,19 +348,21 @@
         on(1, pass_on)
         on(0, near_w)
         on(1, lambda h: stats(3, h))
+        on(3, send_finals)
         on(2, send_parts)
-        on(3, send_finals)
+        on(6, back_relay)
+        on(5, back_y)
         on(4, pairs)
         pl.when(i == last)(lambda: gain_start(0, gain_ref[...]))
-        on(5, back_y)
-        on(6, back_relay)
         on(7, back_home)
         pl.when(i == last + 1)(lambda: gain_start(1, gain_finish(0)))
         pl.when(i == last + 2)(lambda: gain_start(2, gain_finish(1)))
         return carry
 
     lax.fori_loop(0, HEADS_HERE + 7, step, 0)
-    gain_out_ref[...] = gain_finish(2) * (4 * 64 * ROWS) ** (-0.5)
+    gains = gain_finish(2) * (4 * 64 * ROWS) ** (-0.5)
+    gain_q_out[...] = gains[0:1]
+    gain_k_out[...] = gains[1:2]
 
     def drain(h, carry):
         for copy in (to_w, to_h, to_relay, to_y, ret_w, ret_h, ret_relay, ret_y):
@@ -367,14 +382,15 @@
     n = HEADS_HERE
     vmem = pl.BlockSpec(memory_space=pltpu.VMEM)
     smem = pl.BlockSpec(memory_space=pltpu.SMEM)
-    big = jax.ShapeDtypeStruct((ROWS, n * HD), BF16)
+    big = jax.ShapeDtypeStruct((3, ROWS, n * HD), BF16)
+    gain = jax.ShapeDtypeStruct((1, HD), F32)
     sem = pltpu.SemaphoreType.DMA
     return pl.pallas_call(
         attention_kernel,
         name="tile_attention",
-        out_shape=(big, big, big, jax.ShapeDtypeStruct((2, HD), F32)),
+        out_shape=(big, gain, gain),
         in_specs=[smem, smem] + [vmem] * 6,
-        out_specs=(vmem,) * 4,
+        out_specs=(vmem,) * 3,
         scratch_shapes=[
             pltpu.VMEM((5, n, 2, ROWS, HD), BF16),
             pltpu.VMEM((n, 2, ROWS, HD), BF16),
@@ -401,10 +417,11 @@
 
 
 def shards(q_raw, k_raw, values, d_out, gain_q, gain_k, tile_lists, tile_counts):
-    grad_q, grad_k, grad_v, gains = attention(
-        tile_lists[0], tile_counts[0], q_raw[0], k_raw[0], values[0], d_out[0], gain_q[None], gain_k[None]
+    grads, total_q, total_k = attention(
+        jnp.transpose(tile_lists, (2, 0, 1)), tile_counts[0], q_raw[0], k_raw[0], values[0], d_out[0],
+        gain_q[None], gain_k[None],
     )
-    return (grad_q[None], grad_k[None], grad_v[None], gains[0], gains[1])
+    return (grads[0:1], grads[1:2], grads[2:3], total_q[0], total_k[0])
 
 
 def solution(mesh):

time: 160 us -> 155 us (0.969)
  local copies, waits for them, and re-layouts: 6.64 us -> 3.69 us
  Pallas kernels: 152 us -> 150 us
    unnamed x12 -> x6, local copies, waits for them, and re-layouts: 6.13 us -> 1.03 us
    slice x0 -> x1, local copies, waits for them, and re-layouts: none -> 2.66 us  [shards(): return (grads[0:1], grads[1:2], grads[2:3], total_q[0], total_k[0])]
    pallas_call x1, Pallas kernels: 152 us -> 150 us  [attention(): pl.pallas_call(attention_kernel, name='tile_attention', out_shape=(big, g...]
where the time goes in v3:
time: 155 us
  Pallas kernels  150 us (97%)
  local copies, waits for them, and re-layouts  3.69 us (2%)
    pallas_call x1, Pallas kernels, attention(): pl.pallas_call(attention_kernel, name='tile_attention', out_shape=(big, g...  150 us

profile of v3, /device:TPU:1, one launch (start us, length us, event | category | flops | bytes accessed | tf_op | source)
XLA Modules:
  0.0 154.7 jit_solution(18070648173925424707)
XLA Ops:
  0.6 150.3 %tile_attention.1 = (bf16[3,384,768]{2,1,0:T(8,128)(2,1)}, f32[1,128]{1,0:T(1,128)}, f32[1,128]{1,0:T(1,128)}) custom-call(s32[3,1,64]{2,1,0:T(1,128)} %bitcast.14, s32[64]{0:T(128)} %bitcast.15, bf16[384,768]{1,0:T(8,128)(2,1)} %bitcast.10, bf16[384,768]{1,0:T(8,128)(2,1)} %bitcast.11, bf16[384,768]{1,0:T(8,128)(2,1)} %bitcast.12, ...), custom_call_target="tpu_custom_call" | custom-call | tf_op jit(solution)/shard_map/tile_attention/pallas_call | solution.py:388
  151.0 0.0 copy-start.1
  151.0 0.0 copy-start
  151.0 2.7 %fusion = (bf16[1,384,768]{2,1,0:T(8,128)(2,1)}, bf16[1,384,768]{2,1,0:T(8,128)(2,1)}, bf16[1,384,768]{2,1,0:T(8,128)(2,1)}) fusion(bf16[3,384,768]{2,1,0:T(8,128)(2,1)} %get-tuple-element.8), kind=kLoop, calls=%fused_computation | loop fusion | bytes 3538944 | tf_op jit(solution)/shard_map/slice | solution.py:424
  153.7 0.0 copy-done.1
  153.7 0.5 copy.15
  154.2 0.0 copy-done
  154.2 0.5 copy.16
Async XLA Ops:
  151.0 2.7 %copy-start.1 = (f32[1,128]{1,0:T(1,128)S(1)}, f32[1,128]{1,0:T(1,128)}, u32[]{:S(2)}) copy-start(f32[1,128]{1,0:T(1,128)} %get-tuple-element.9) | copy-start | bytes 1540
  151.0 3.2 %copy-start = (f32[1,128]{1,0:T(1,128)S(1)}, f32[1,128]{1,0:T(1,128)}, u32[]{:S(2)}) copy-start(f32[1,128]{1,0:T(1,128)} %get-tuple-element.10) | copy-start | bytes 1540

commit v4 on v3

--- a/solution.py
+++ b/solution.py
@@ -47,11 +47,11 @@
 
 
 def attention_kernel(
-    lists, counts, q_ref, k_ref, v_ref, g_ref, gain_q_ref, gain_k_ref,
+    lists, counts, q_hbm, k_hbm, v_hbm, g_hbm, gain_q_ref, gain_k_ref,
     grads_ref, gain_q_out, gain_k_out,
     slots, keys, key_t, part_out, part_in, final_out, final_in, dq32, dq_out, ret_in, ds_ref, dk_acc, dv_acc,
-    gain_ref, gain_a, gain_b, gain_c,
-    slot_send, slot_recv, part_send, part_recv, final_send, final_recv, ret_send, ret_recv, gain_send, gain_recv,
+    gain_ref, gain_a, gain_b, gain_c, q_ref, k_ref,
+    slot_send, slot_recv, part_send, part_recv, final_send, final_recv, ret_send, ret_recv, gain_send, gain_recv, load_sem,
 ):
     factor = HD ** (-0.5)
     scale2 = factor * LOG2E
@@ -85,17 +85,30 @@
     def lanes(h):
         return pl.ds(pl.multiple_of(h * HD, HD), HD)
 
+    def load_g(h):
+        return pltpu.make_async_copy(g_hbm.at[:, lanes(h)], slots.at[0, h, 1], load_sem.at[0, h])
+
+    def load_v(h):
+        return pltpu.make_async_copy(v_hbm.at[:, lanes(h)], keys.at[h, 1], load_sem.at[1, h])
+
+    load_q = pltpu.make_async_copy(q_hbm, q_ref, load_sem.at[2, 0])
+    load_k = pltpu.make_async_copy(k_hbm, k_ref, load_sem.at[2, 1])
+    load_q.start()
+    for h in range(HEADS_HERE):
+        load_g(h).start()
+    load_k.start()
+    for h in range(HEADS_HERE):
+        load_v(h).start()
+
     def prepare_q(h, carry):
         wide = q_ref[:, lanes(h)].astype(F32)
         slots[0, h, 0] = (wide * inverse_norm(wide) * gain_q_ref[...]).astype(BF16)
-        slots[0, h, 1] = g_ref[:, lanes(h)]
         return carry
 
     def prepare_k(h, carry):
         wide = k_ref[:, lanes(h)].astype(F32)
         key = (wide * inverse_norm(wide) * gain_k_ref[...]).astype(BF16)
         keys[h, 0] = key
-        keys[h, 1] = v_ref[:, lanes(h)]
         key_t[h] = key.astype(F32).T.astype(BF16)
         return carry
 
@@ -269,13 +282,21 @@
         return value
 
     gain_ref[...] = jnp.zeros_like(gain_ref)
-    lax.fori_loop(0, HEADS_HERE, prepare_q, 0)
-    pl.semaphore_wait(barrier, 7 + 3 * (RING - 1))
-    to_h(0).start()
-    to_w(0).start()
-    to_h(1).start()
-    to_h(2).start()
+    load_q.wait()
+    for h in range(3):
+        prepare_q(h, 0)
+        load_g(h).wait()
+        if h == 0:
+            pl.semaphore_wait(barrier, 7 + 3 * (RING - 1))
+            to_w(h).start()
+        to_h(h).start()
+    lax.fori_loop(3, HEADS_HERE, prepare_q, 0)
+    for h in range(3, HEADS_HERE):
+        load_g(h).wait()
+    load_k.wait()
     lax.fori_loop(0, HEADS_HERE, prepare_k, 0)
+    for h in range(HEADS_HERE):
+        load_v(h).wait()
 
     last = HEADS_HERE + 3
 
@@ -351,12 +372,12 @@
         on(3, send_finals)
         on(2, send_parts)
         on(6, back_relay)
+        pl.when(i == last + 2)(lambda: gain_start(2, gain_finish(1)))
         on(5, back_y)
+        pl.when(i == last + 1)(lambda: gain_start(1, gain_finish(0)))
         on(4, pairs)
         pl.when(i == last)(lambda: gain_start(0, gain_ref[...]))
         on(7, back_home)
-        pl.when(i == last + 1)(lambda: gain_start(1, gain_finish(0)))
-        pl.when(i == last + 2)(lambda: gain_start(2, gain_finish(1)))
         return carry
 
     lax.fori_loop(0, HEADS_HERE + 7, step, 0)
@@ -382,6 +403,7 @@
     n = HEADS_HERE
     vmem = pl.BlockSpec(memory_space=pltpu.VMEM)
     smem = pl.BlockSpec(memory_space=pltpu.SMEM)
+    hbm = pl.BlockSpec(memory_space=pltpu.HBM)
     big = jax.ShapeDtypeStruct((3, ROWS, n * HD), BF16)
     gain = jax.ShapeDtypeStruct((1, HD), F32)
     sem = pltpu.SemaphoreType.DMA
@@ -389,7 +411,7 @@
         attention_kernel,
         name="tile_attention",
         out_shape=(big, gain, gain),
-        in_specs=[smem, smem] + [vmem] * 6,
+        in_specs=[smem, smem] + [hbm] * 4 + [vmem] * 2,
         out_specs=(vmem,) * 3,
         scratch_shapes=[
             pltpu.VMEM((5, n, 2, ROWS, HD), BF16),
@@ -409,8 +431,10 @@
             pltpu.VMEM((RING, 2, HD), F32),
             pltpu.VMEM((RING, 2, HD), F32),
             pltpu.VMEM((RING, 2, HD), F32),
+            pltpu.VMEM((ROWS, n * HD), BF16),
+            pltpu.VMEM((ROWS, n * HD), BF16),
             sem((4, n)), sem((4, n)), sem((5, n)), sem((5, n)), sem((5, n)), sem((5, n)), sem((4, n)), sem((4, n)),
-            sem((3, RING)), sem((3, RING)),
+            sem((3, RING)), sem((3, RING)), sem((3, n)),
         ],
         compiler_params=pltpu.CompilerParams(collective_id=1, has_side_effects=True, vmem_limit_bytes=56 * 2**20),
     )(lists, counts, q, k, v, g, gain_q, gain_k)

time: 155 us -> 155 us (level)
  no operation moved by 1% of the time
where the time goes in v4:
time: 155 us; the launch traced here: 154 us
  Pallas kernels  150 us (97%)
  local copies, waits for them, and re-layouts  3.69 us (2%)
    pallas_call x1, Pallas kernels, attention(): pl.pallas_call(attention_kernel, name='tile_attention', out_shape=(big, g...  150 us

profile of v4, /device:TPU:1, one launch (start us, length us, event | category | flops | bytes accessed | tf_op | source)
XLA Modules:
  0.0 154.4 jit_solution(12739656722783152303)
XLA Ops:
  0.6 150.1 %tile_attention.1 = (bf16[3,384,768]{2,1,0:T(8,128)(2,1)}, f32[1,128]{1,0:T(1,128)}, f32[1,128]{1,0:T(1,128)}) custom-call(s32[3,1,64]{2,1,0:T(1,128)} %bitcast.14, s32[64]{0:T(128)} %bitcast.15, bf16[384,768]{1,0:T(8,128)(2,1)} %bitcast.10, bf16[384,768]{1,0:T(8,128)(2,1)} %bitcast.11, bf16[384,768]{1,0:T(8,128)(2,1)} %bitcast.12, ...), custom_call_target="tpu_custom_call" | custom-call | tf_op jit(solution)/shard_map/tile_attention/pallas_call | solution.py:410
  150.7 0.0 copy-start.1
  150.7 0.0 copy-start
  150.7 2.7 %fusion = (bf16[1,384,768]{2,1,0:T(8,128)(2,1)}, bf16[1,384,768]{2,1,0:T(8,128)(2,1)}, bf16[1,384,768]{2,1,0:T(8,128)(2,1)}) fusion(bf16[3,384,768]{2,1,0:T(8,128)(2,1)} %get-tuple-element.8), kind=kLoop, calls=%fused_computation | loop fusion | bytes 3538944 | tf_op jit(solution)/shard_map/slice | solution.py:448
  153.4 0.0 copy-done.1
  153.4 0.5 copy.15
  153.9 0.0 copy-done
  153.9 0.5 copy.16
Async XLA Ops:
  150.7 2.7 %copy-start.1 = (f32[1,128]{1,0:T(1,128)S(1)}, f32[1,128]{1,0:T(1,128)}, u32[]{:S(2)}) copy-start(f32[1,128]{1,0:T(1,128)} %get-tuple-element.9) | copy-start | bytes 1540
  150.7 3.2 %copy-start = (f32[1,128]{1,0:T(1,128)S(1)}, f32[1,128]{1,0:T(1,128)}, u32[]{:S(2)}) copy-start(f32[1,128]{1,0:T(1,128)} %get-tuple-element.10) | copy-start | bytes 1540

commit v5 on v4

--- a/solution.py
+++ b/solution.py
@@ -322,6 +322,7 @@
 
             stats(0, h)
             stats(2, h)
+            part_copy(2, h).start()
 
         def pass_on(h):
             to_relay(h).wait_recv()
@@ -330,12 +331,16 @@
         def near_w(h):
             to_w(h).wait_recv()
             stats(1, h)
+            part_copy(1, h).start()
+
+        def far_t(h):
+            stats(3, h)
+            part_copy(3, h).start()
 
         def send_parts(h):
             to_y(h).wait_recv()
             stats(4, h)
-            for place in range(1, NEAR + 1):
-                part_copy(place, h).start()
+            part_copy(4, h).start()
 
         def pairs(h):
             for place in range(1, NEAR + 1):
@@ -368,7 +373,7 @@
         on(0, arrive)
         on(1, pass_on)
         on(0, near_w)
-        on(1, lambda h: stats(3, h))
+        on(1, far_t)
         on(3, send_finals)
         on(2, send_parts)
         on(6, back_relay)

time: 155 us -> 156 us (level)
  no operation moved by 1% of the time
where the time goes in v5:
time: 156 us; the launch traced here: 155 us
  Pallas kernels  151 us (97%)
  local copies, waits for them, and re-layouts  3.69 us (2%)
    pallas_call x1, Pallas kernels, attention(): pl.pallas_call(attention_kernel, name='tile_attention', out_shape=(big, g...  151 us

profile of v5, /device:TPU:1, one launch (start us, length us, event | category | flops | bytes accessed | tf_op | source)
XLA Modules:
  0.0 155.1 jit_solution(12748885708904303014)
XLA Ops:
  0.6 150.8 %tile_attention.1 = (bf16[3,384,768]{2,1,0:T(8,128)(2,1)}, f32[1,128]{1,0:T(1,128)}, f32[1,128]{1,0:T(1,128)}) custom-call(s32[3,1,64]{2,1,0:T(1,128)} %bitcast.14, s32[64]{0:T(128)} %bitcast.15, bf16[384,768]{1,0:T(8,128)(2,1)} %bitcast.10, bf16[384,768]{1,0:T(8,128)(2,1)} %bitcast.11, bf16[384,768]{1,0:T(8,128)(2,1)} %bitcast.12, ...), custom_call_target="tpu_custom_call" | custom-call | tf_op jit(solution)/shard_map/tile_attention/pallas_call | solution.py:415
  151.4 0.0 copy-start.1
  151.4 0.0 copy-start
  151.4 2.7 %fusion = (bf16[1,384,768]{2,1,0:T(8,128)(2,1)}, bf16[1,384,768]{2,1,0:T(8,128)(2,1)}, bf16[1,384,768]{2,1,0:T(8,128)(2,1)}) fusion(bf16[3,384,768]{2,1,0:T(8,128)(2,1)} %get-tuple-element.8), kind=kLoop, calls=%fused_computation | loop fusion | bytes 3538944 | tf_op jit(solution)/shard_map/slice | solution.py:453
  154.1 0.0 copy-done.1
  154.1 0.5 copy.15
  154.6 0.0 copy-done
  154.6 0.5 copy.16
Async XLA Ops:
  151.4 2.7 %copy-start.1 = (f32[1,128]{1,0:T(1,128)S(1)}, f32[1,128]{1,0:T(1,128)}, u32[]{:S(2)}) copy-start(f32[1,128]{1,0:T(1,128)} %get-tuple-element.9) | copy-start | bytes 1540
  151.4 3.2 %copy-start = (f32[1,128]{1,0:T(1,128)S(1)}, f32[1,128]{1,0:T(1,128)}, u32[]{:S(2)}) copy-start(f32[1,128]{1,0:T(1,128)} %get-tuple-element.10) | copy-start | bytes 1540
